TPU v7x, 32 devices: a whole 2x2x4 slice. The times are simulated.
32 devices in a mesh: batch: 2 (over x), space: 16 (over z, y, core).
Axes of the slice: x: 2, y: 2, z: 4, core: 2. Of those that a mesh axis runs over, the one named last changes fastest.
Arguments:
- courant: float32 [128, 16, 256], P('space'), may hold values from 0.06 to 0.18
- wavelet: float32 [2, 64, 7], P('batch'), may hold values from -6 to 6
- source_owner: int32 [2, 64], P('batch'), may hold values from 0 to 15
- source_cell: int32 [2, 64], P('batch'), may hold values from 0 to 32767
- traces: float32 [2, 4096, 7], P('batch', 'space'), may hold values from -6 to 6
- station_owner: int32 [2, 4096, 1], P('batch', 'space'), may hold values from 0 to 15; in each aligned block of 256 rows (0 to 255, 256 to 511, ..., all dimensions but the last counted through in order) at most 32 rows name the same one
- station_cell: int32 [2, 4096], P('batch', 'space'), may hold values from 0 to 32767
Outputs:
- update: float32 [128, 16, 256], P('space', 'batch')
- agreement: float32 [1], replicated
Inputs may be any that keep to these rules, and one draw needn't show every extreme that they name: `station_owner`: among the 256 trace rows of one device, at most 32 name the same owner, and in every draw some device reaches 32 for some owner.
All inputs are finite; a program needn't handle non-finite values.
Results may differ from a plain program's by a relative error of at most 0.0003.
Values sent between devices are 32-bit elements; how exact they have to be, the bound alone decides.
A program may use at most 64 MiB of HBM per device.

v0:
```python
import jax
import jax.numpy as jnp
from jax import lax
from jax.sharding import PartitionSpec as P

center_tap = -205.0 / 72.0
stencil_taps = (1.6, -0.2, 8.0 / 315.0, -1.0 / 560.0)
epsilon = 1e-06


def padded(array, sides, width):
    for axis, dim in sides:
        peers, length = (lax.axis_size(axis), array.shape[dim])
        up = [(i, (i + 1) % peers) for i in range(peers - 1)]
        down = [(j, i) for i, j in up]
        last = lax.slice_in_dim(array, length - width, length, axis=dim)
        initial = lax.slice_in_dim(array, 0, width, axis=dim)
        before = lax.ppermute(last, axis, up)
        after = lax.ppermute(initial, axis, down)
        array = jnp.concatenate([before, array, after], axis=dim)
    return array


def laplace_rows(extended, height):
    span_y = extended.shape[1] - 8
    span_z = extended.shape[2] - 8

    def window(first, second, third):
        return extended[first : first + height, second : second + span_y, third : third + span_z]

    accumulated = 3.0 * center_tap * window(4, 4, 4)
    for offset in range(1, 5):
        neighbours = window(4 + offset, 4, 4) + window(4 - offset, 4, 4)
        neighbours = neighbours + window(4, 4 + offset, 4) + window(4, 4 - offset, 4)
        neighbours = neighbours + window(4, 4, 4 + offset) + window(4, 4, 4 - offset)
        accumulated = accumulated + stencil_taps[offset - 1] * neighbours
    return accumulated


def pad_across(slab_block):
    return jnp.pad(slab_block, ((0, 0), (4, 4), (4, 4)))


def stencil(wave_field):
    width_x = wave_field.shape[0]
    rimmed = padded(wave_field, (("space", 0),), 4)
    return laplace_rows(pad_across(rimmed), width_x)


def inject(wave_field, positions, amounts):
    flattened = wave_field.reshape(-1)
    return flattened.at[positions].add(amounts).reshape(wave_field.shape)


def body(courant, wavelet, source_owner, source_cell, traces, station_owner, station_cell):
    width_x, width_y, width_z = courant.shape
    columns = traces.shape[2]
    position = lax.axis_index("space")
    parties = lax.axis_size("space")
    inside = source_owner[0] == position
    source_flat = jnp.where(inside, source_cell[0], 0)
    source_amount = jnp.where(inside[:, None], wavelet[0], 0.0)
    owners = station_owner[0, :, 0]
    capacity = max(2 * traces.shape[1] // parties, 4)
    matches = (owners[:, None] == jnp.arange(parties, dtype=jnp.int32)[None, :]).astype(jnp.int32)
    ranking = jnp.sum((jnp.cumsum(matches, axis=0) - 1) * matches, axis=1)
    slot_index = owners * capacity + ranking
    sent_values = (
        jnp.zeros((parties * capacity, columns), jnp.float32).at[slot_index].set(traces[0])
    )
    sent_cells = (
        jnp.full((parties * capacity,), -1.0, jnp.float32)
        .at[slot_index]
        .set(station_cell[0].astype(jnp.float32))
    )
    got_values, got_cells = (
        lax.all_to_all(sent_values, "space", split_axis=0, concat_axis=0, tiled=True),
        lax.all_to_all(sent_cells, "space", split_axis=0, concat_axis=0, tiled=True),
    )
    usable = got_cells >= 0.0
    station_local = jnp.where(usable, got_cells.astype(jnp.int32), 0)
    station_amount = jnp.where(usable[:, None], got_values, 0.0)
    zero_field = jnp.zeros((width_x, width_y, width_z), jnp.float32)
    snapshots = [zero_field, inject(zero_field, source_flat, source_amount[:, 0])]
    for moment in range(1, columns):
        current = snapshots[moment]
        following = 2.0 * current - snapshots[moment - 1] + courant * stencil(current)
        snapshots.append(inject(following, source_flat, source_amount[:, moment]))
    adjoint = inject(zero_field, station_local, station_amount[:, columns - 1])
    previous_adjoint = zero_field
    gradient = adjoint * (
        snapshots[columns] - 2.0 * snapshots[columns - 1] + snapshots[columns - 2]
    )
    for moment in range(columns - 2, 0, -1):
        newer = 2.0 * adjoint - previous_adjoint + stencil(courant * adjoint)
        newer = inject(newer, station_local, station_amount[:, moment])
        previous_adjoint, adjoint = (adjoint, newer)
        gradient = gradient + adjoint * (
            snapshots[moment + 1] - 2.0 * snapshots[moment] + snapshots[moment - 1]
        )
    halves = lax.all_to_all(gradient[None], "batch", split_axis=2, concat_axis=0, tiled=True)
    summed = halves[0] + halves[1]
    norm_first, norm_second = lax.psum(
        (jnp.sum(halves[0] * halves[0]), jnp.sum(halves[1] * halves[1])), ("batch", "space")
    )
    cells = float(width_x * width_y * width_z * parties)
    mean_first = norm_first / cells
    mean_second = norm_second / cells
    update = summed / jnp.sqrt((mean_first + mean_second) / 2.0 + epsilon)
    share = (mean_first + epsilon) / (mean_first + mean_second + 2.0 * epsilon)
    return (update, jnp.stack([share]))


def solution(mesh):
    return jax.shard_map(
        body,
        mesh=mesh,
        in_specs=(
            P("space", None, None),
            P("batch", None, None),
            P("batch", None),
            P("batch", None),
            P("batch", "space", None),
            P("batch", "space", None),
            P("batch", "space"),
        ),
        out_specs=(P("space", "batch", None), P()),
        check_vma=False,
    )
```

profile of v0, /device:TPU:0, one launch (start us, length us, event | category | flops | bytes accessed | tf_op | source)
XLA Modules:
  0.0 185.0 jit_solution(4671132146378197326)
XLA Ops:
  5.0 7.4 %all-to-all-start = ((f32[16,32,1]{1,2,0:T(1,128)}), f32[16,32,1]{1,2,0:T(1,128)S(1)}, u32[]{:S(2)}, u32[]{:S(2)}) async-start(f32[16,32,1]{1,2,0:T(1,128)} %bitcast.7), calls=%async_computation | async-start | bytes 16384 | tf_op jit(solution)/shard_map/all_to_all | solution.py:78
  14.8 2.3 %collective-permute-start.1 = (f32[4,16,256]{2,1,0:T(8,128)S(1)}, f32[4,16,256]{2,1,0:T(8,128)S(1)}, u32[]{:S(2)}, u32[]{:S(2)}) collective-permute-start(f32[4,16,256]{2,1,0:T(8,128)S(1)} %slice.1253), channel_id=1, source_target_pairs={{0,1},{1,2},{2,3},{3,4},{4,5},{5,6},{6,7},{7,8},{8,9},{9,10},{10,1... | collective-permute-start | bytes 196616 | tf_op jit(solution)/shard_map/ppermute | solution.py:18
  21.4 8.0 %all-to-all-start.1 = ((f32[16,1,224]{2,1,0:T(1,128)}), f32[16,1,224]{2,1,0:T(1,128)S(1)}, u32[]{:S(2)}, u32[]{:S(2)}) async-start(f32[16,1,224]{2,1,0:T(1,128)} %reshape.760), calls=%async_computation.1 | async-start | bytes 32768 | tf_op jit(solution)/shard_map/all_to_all | solution.py:77
  29.7 6.2 %all-to-all-done.1 = f32[16,1,224]{2,1,0:T(1,128)S(1)} async-done(((f32[16,1,224]{2,1,0:T(1,128)}), f32[16,1,224]{2,1,0:T(1,128)S(1)}, u32[]{:S(2)}, u32[]{:S(2)}) %all-to-all-start.1) | async-done | bytes 14368 | tf_op jit(solution)/shard_map/all_to_all | solution.py:77
  38.5 3.3 %scatter_custom_fusion.2 = f32[32768]{0:T(1024)S(1)} fusion(s32[512]{0:T(512)S(1)} %bitcast.117, f32[512]{0:T(512)S(1)} %get-tuple-element.7, f32[]{:T(128)} %constant.18.clone.1), kind=kCustom, calls=%fused_computation.486 | custom fusion | flops 512 | bytes 131076 | tf_op jit(solution)/shard_map/scatter-add | solution.py:52
  44.1 3.0 %collective-permute-start.13 = (f32[4,16,256]{2,1,0:T(8,128)S(1)}, f32[4,16,256]{2,1,0:T(8,128)S(1)}, u32[]{:S(2)}, u32[]{:S(2)}) collective-permute-start(f32[4,16,256]{2,1,0:T(8,128)S(1)} %get-tuple-element.45), channel_id=1, source_target_pairs={{0,1},{1,2},{2,3},{3,4},{4,5},{5,6},{6,7},{7,8},{8,9},{9,10},{10,1... | collective-permute-start | bytes 196616 | tf_op jit(solution)/shard_map/ppermute | solution.py:18
  49.3 3.1 %collective-permute-start.3 = (f32[4,16,256]{2,1,0:T(8,128)S(1)}, f32[4,16,256]{2,1,0:T(8,128)S(1)}, u32[]{:S(2)}, u32[]{:S(2)}) collective-permute-start(f32[4,16,256]{2,1,0:T(8,128)S(1)} %slice.1282), channel_id=1, source_target_pairs={{0,1},{1,2},{2,3},{3,4},{4,5},{5,6},{6,7},{7,8},{8,9},{9,10},{10,1... | collective-permute-start | bytes 196616 | tf_op jit(solution)/shard_map/ppermute | solution.py:18
  54.6 3.4 %scatter_fusion.6 = f32[32768]{0:T(1024)S(1)} fusion(f32[32768]{0:T(1024)S(1)} %bitcast.90, s32[512]{0:T(512)S(1)} %bitcast.118, f32[512]{0:T(512)S(1)} %get-tuple-element.6), kind=kCustom, calls=%fused_computation.10 | custom fusion | flops 512 | bytes 8192 | tf_op jit(solution)/shard_map/scatter-add | solution.py:52
  59.5 3.8 %collective-permute-start.15 = (f32[4,16,256]{2,1,0:T(8,128)S(1)}, f32[4,16,256]{2,1,0:T(8,128)S(1)}, u32[]{:S(2)}, u32[]{:S(2)}) collective-permute-start(f32[4,16,256]{2,1,0:T(8,128)S(1)} %get-tuple-element.43), channel_id=1, source_target_pairs={{0,1},{1,2},{2,3},{3,4},{4,5},{5,6},{6,7},{7,8},{8,9},{9,10},{10,1... | collective-permute-start | bytes 196616 | tf_op jit(solution)/shard_map/ppermute | solution.py:18
  65.5 3.6 %collective-permute-start.5 = (f32[4,16,256]{2,1,0:T(8,128)S(1)}, f32[4,16,256]{2,1,0:T(8,128)S(1)}, u32[]{:S(2)}, u32[]{:S(2)}) collective-permute-start(f32[4,16,256]{2,1,0:T(8,128)S(1)} %slice.1311), channel_id=1, source_target_pairs={{0,1},{1,2},{2,3},{3,4},{4,5},{5,6},{6,7},{7,8},{8,9},{9,10},{10,1... | collective-permute-start | bytes 196616 | tf_op jit(solution)/shard_map/ppermute | solution.py:18
  69.2 1.5 collective-permute-start.4
  71.6 3.4 %scatter_fusion.7 = f32[32768]{0:T(1024)S(1)} fusion(f32[32768]{0:T(1024)S(1)} %bitcast.91, s32[512]{0:T(512)S(1)} %bitcast.119, f32[512]{0:T(512)S(1)} %get-tuple-element.5), kind=kCustom, calls=%fused_computation.11 | custom fusion | flops 512 | bytes 8192 | tf_op jit(solution)/shard_map/scatter-add | solution.py:52
  76.5 3.8 %collective-permute-start.17 = (f32[4,16,256]{2,1,0:T(8,128)S(1)}, f32[4,16,256]{2,1,0:T(8,128)S(1)}, u32[]{:S(2)}, u32[]{:S(2)}) collective-permute-start(f32[4,16,256]{2,1,0:T(8,128)S(1)} %get-tuple-element.41), channel_id=1, source_target_pairs={{0,1},{1,2},{2,3},{3,4},{4,5},{5,6},{6,7},{7,8},{8,9},{9,10},{10,1... | collective-permute-start | bytes 196616 | tf_op jit(solution)/shard_map/ppermute | solution.py:18
  82.5 3.7 %collective-permute-start.7 = (f32[4,16,256]{2,1,0:T(8,128)S(1)}, f32[4,16,256]{2,1,0:T(8,128)S(1)}, u32[]{:S(2)}, u32[]{:S(2)}) collective-permute-start(f32[4,16,256]{2,1,0:T(8,128)S(1)} %slice.1340), channel_id=1, source_target_pairs={{0,1},{1,2},{2,3},{3,4},{4,5},{5,6},{6,7},{7,8},{8,9},{9,10},{10,1... | collective-permute-start | bytes 196616 | tf_op jit(solution)/shard_map/ppermute | solution.py:18
  88.5 3.4 %scatter_fusion.8 = f32[32768]{0:T(1024)S(1)} fusion(f32[32768]{0:T(1024)S(1)} %bitcast.92, s32[512]{0:T(512)S(1)} %bitcast.120, f32[512]{0:T(512)S(1)} %get-tuple-element.4), kind=kCustom, calls=%fused_computation.12 | custom fusion | flops 512 | bytes 8192 | tf_op jit(solution)/shard_map/scatter-add | solution.py:52
  93.4 3.9 %collective-permute-start.19 = (f32[4,16,256]{2,1,0:T(8,128)S(1)}, f32[4,16,256]{2,1,0:T(8,128)S(1)}, u32[]{:S(2)}, u32[]{:S(2)}) collective-permute-start(f32[4,16,256]{2,1,0:T(8,128)S(1)} %get-tuple-element.39), channel_id=1, source_target_pairs={{0,1},{1,2},{2,3},{3,4},{4,5},{5,6},{6,7},{7,8},{8,9},{9,10},{10,1... | collective-permute-start | bytes 196616 | tf_op jit(solution)/shard_map/ppermute | solution.py:18
  99.4 4.6 %collective-permute-start.9 = (f32[4,16,256]{2,1,0:T(8,128)S(1)}, f32[4,16,256]{2,1,0:T(8,128)S(1)}, u32[]{:S(2)}, u32[]{:S(2)}) collective-permute-start(f32[4,16,256]{2,1,0:T(8,128)S(1)} %slice.1369), channel_id=1, source_target_pairs={{0,1},{1,2},{2,3},{3,4},{4,5},{5,6},{6,7},{7,8},{8,9},{9,10},{10,1... | collective-permute-start | bytes 196616 | tf_op jit(solution)/shard_map/ppermute | solution.py:18
  106.3 3.4 %scatter_fusion.9 = f32[32768]{0:T(1024)S(1)} fusion(f32[32768]{0:T(1024)S(1)} %bitcast.93, s32[512]{0:T(512)S(1)} %bitcast.121, f32[512]{0:T(512)S(1)} %get-tuple-element.3), kind=kCustom, calls=%fused_computation.13 | custom fusion | flops 512 | bytes 8192 | tf_op jit(solution)/shard_map/scatter-add | solution.py:52
  111.2 3.9 %collective-permute-start.21 = (f32[4,16,256]{2,1,0:T(8,128)S(1)}, f32[4,16,256]{2,1,0:T(8,128)S(1)}, u32[]{:S(2)}, u32[]{:S(2)}) collective-permute-start(f32[4,16,256]{2,1,0:T(8,128)S(1)} %get-tuple-element.37), channel_id=1, source_target_pairs={{0,1},{1,2},{2,3},{3,4},{4,5},{5,6},{6,7},{7,8},{8,9},{9,10},{10,1... | collective-permute-start | bytes 196616 | tf_op jit(solution)/shard_map/ppermute | solution.py:18
  117.2 4.7 %collective-permute-start.11 = (f32[4,16,256]{2,1,0:T(8,128)S(1)}, f32[4,16,256]{2,1,0:T(8,128)S(1)}, u32[]{:S(2)}, u32[]{:S(2)}) collective-permute-start(f32[4,16,256]{2,1,0:T(8,128)S(1)} %slice.1398), channel_id=1, source_target_pairs={{0,1},{1,2},{2,3},{3,4},{4,5},{5,6},{6,7},{7,8},{8,9},{9,10},{10,1... | collective-permute-start | bytes 196616 | tf_op jit(solution)/shard_map/ppermute | solution.py:18
  122.0 1.5 collective-permute-start.10
  124.5 3.4 %scatter_fusion.10 = f32[32768]{0:T(1024)S(1)} fusion(f32[32768]{0:T(1024)S(1)} %bitcast.94, s32[512]{0:T(512)S(1)} %bitcast.122, f32[512]{0:T(512)S(1)} %get-tuple-element.2), kind=kCustom, calls=%fused_computation.14 | custom fusion | flops 512 | bytes 8192 | tf_op jit(solution)/shard_map/scatter-add | solution.py:52
  130.3 7.5 %all_to_all.36 = f32[1,8,16,256]{3,1,0,2:T(8,128)S(1)} all-to-all(f32[1,8,16,256]{3,1,0,2:T(8,128)S(1)} %copy.22), channel_id=1, replica_groups=mesh['batch'=2,'space'=16] {'batch'}, dimensions={2} | all-to-all | bytes 262144 | tf_op jit(solution)/shard_map/all_to_all | solution.py:101
  138.5 43.4 %all-reduce.11 = (f32[]{:T(128)}, f32[]{:T(128)}) all-reduce(f32[]{:T(128)} %get-tuple-element.9, f32[]{:T(128)} %get-tuple-element.8), channel_id=1, replica_groups=mesh['batch'=2,'space'=16] {'batch','space'}, use_global_device_ids=true, to_apply=%region_19.20 | all-reduce | flops 2 | bytes 16 | tf_op jit(solution)/shard_map/psum | solution.py:103
  (190 shorter events, 44.1 us)
Async XLA Ops:
  5.0 16.5 %all-to-all-start = ((f32[16,32,1]{1,2,0:T(1,128)}), f32[16,32,1]{1,2,0:T(1,128)S(1)}, u32[]{:S(2)}, u32[]{:S(2)}) async-start(f32[16,32,1]{1,2,0:T(1,128)} %bitcast.7), calls=%async_computation | async-start | bytes 16384 | tf_op jit(solution)/shard_map/all_to_all | solution.py:78
  14.8 32.3 %collective-permute-start.1 = (f32[4,16,256]{2,1,0:T(8,128)S(1)}, f32[4,16,256]{2,1,0:T(8,128)S(1)}, u32[]{:S(2)}, u32[]{:S(2)}) collective-permute-start(f32[4,16,256]{2,1,0:T(8,128)S(1)} %slice.1253), channel_id=1, source_target_pairs={{0,1},{1,2},{2,3},{3,4},{4,5},{5,6},{6,7},{7,8},{8,9},{9,10},{10,1... | collective-permute-start | bytes 196616 | tf_op jit(solution)/shard_map/ppermute | solution.py:18
  17.1 30.0 %collective-permute-start = (f32[4,16,256]{2,1,0:T(8,128)S(1)}, f32[4,16,256]{2,1,0:T(8,128)S(1)}, u32[]{:S(2)}, u32[]{:S(2)}) collective-permute-start(f32[4,16,256]{2,1,0:T(8,128)S(1)} %slice.1250), channel_id=1, source_target_pairs={{1,0},{2,1},{3,2},{4,3},{5,4},{6,5},{7,6},{8,7},{9,8},{10,9},{11,1... | collective-permute-start | bytes 196616 | tf_op jit(solution)/shard_map/ppermute | solution.py:19
  21.4 14.5 %all-to-all-start.1 = ((f32[16,1,224]{2,1,0:T(1,128)}), f32[16,1,224]{2,1,0:T(1,128)S(1)}, u32[]{:S(2)}, u32[]{:S(2)}) async-start(f32[16,1,224]{2,1,0:T(1,128)} %reshape.760), calls=%async_computation.1 | async-start | bytes 32768 | tf_op jit(solution)/shard_map/all_to_all | solution.py:77
  42.8 10.9 %collective-permute-start.12 = (f32[4,16,256]{2,1,0:T(8,128)S(1)}, f32[4,16,256]{2,1,0:T(8,128)S(1)}, u32[]{:S(2)}, u32[]{:S(2)}) collective-permute-start(f32[4,16,256]{2,1,0:T(8,128)S(1)} %get-tuple-element.44), channel_id=1, source_target_pairs={{1,0},{2,1},{3,2},{4,3},{5,4},{6,5},{7,6},{8,7},{9,8},{10,9},{11,1... | collective-permute-start | bytes 196616 | tf_op jit(solution)/shard_map/ppermute | solution.py:19
  44.1 9.6 %collective-permute-start.13 = (f32[4,16,256]{2,1,0:T(8,128)S(1)}, f32[4,16,256]{2,1,0:T(8,128)S(1)}, u32[]{:S(2)}, u32[]{:S(2)}) collective-permute-start(f32[4,16,256]{2,1,0:T(8,128)S(1)} %get-tuple-element.45), channel_id=1, source_target_pairs={{0,1},{1,2},{2,3},{3,4},{4,5},{5,6},{6,7},{7,8},{8,9},{9,10},{10,1... | collective-permute-start | bytes 196616 | tf_op jit(solution)/shard_map/ppermute | solution.py:18
  49.3 14.0 %collective-permute-start.3 = (f32[4,16,256]{2,1,0:T(8,128)S(1)}, f32[4,16,256]{2,1,0:T(8,128)S(1)}, u32[]{:S(2)}, u32[]{:S(2)}) collective-permute-start(f32[4,16,256]{2,1,0:T(8,128)S(1)} %slice.1282), channel_id=1, source_target_pairs={{0,1},{1,2},{2,3},{3,4},{4,5},{5,6},{6,7},{7,8},{8,9},{9,10},{10,1... | collective-permute-start | bytes 196616 | tf_op jit(solution)/shard_map/ppermute | solution.py:18
  52.4 11.0 %collective-permute-start.2 = (f32[4,16,256]{2,1,0:T(8,128)S(1)}, f32[4,16,256]{2,1,0:T(8,128)S(1)}, u32[]{:S(2)}, u32[]{:S(2)}) collective-permute-start(f32[4,16,256]{2,1,0:T(8,128)S(1)} %slice.1279), channel_id=1, source_target_pairs={{1,0},{2,1},{3,2},{4,3},{5,4},{6,5},{7,6},{8,7},{9,8},{10,9},{11,1... | collective-permute-start | bytes 196616 | tf_op jit(solution)/shard_map/ppermute | solution.py:19
  58.2 12.5 %collective-permute-start.14 = (f32[4,16,256]{2,1,0:T(8,128)S(1)}, f32[4,16,256]{2,1,0:T(8,128)S(1)}, u32[]{:S(2)}, u32[]{:S(2)}) collective-permute-start(f32[4,16,256]{2,1,0:T(8,128)S(1)} %get-tuple-element.42), channel_id=1, source_target_pairs={{1,0},{2,1},{3,2},{4,3},{5,4},{6,5},{7,6},{8,7},{9,8},{10,9},{11,1... | collective-permute-start | bytes 196616 | tf_op jit(solution)/shard_map/ppermute | solution.py:19
  59.5 11.2 %collective-permute-start.15 = (f32[4,16,256]{2,1,0:T(8,128)S(1)}, f32[4,16,256]{2,1,0:T(8,128)S(1)}, u32[]{:S(2)}, u32[]{:S(2)}) collective-permute-start(f32[4,16,256]{2,1,0:T(8,128)S(1)} %get-tuple-element.43), channel_id=1, source_target_pairs={{0,1},{1,2},{2,3},{3,4},{4,5},{5,6},{6,7},{7,8},{8,9},{9,10},{10,1... | collective-permute-start | bytes 196616 | tf_op jit(solution)/shard_map/ppermute | solution.py:18
  65.5 14.8 %collective-permute-start.5 = (f32[4,16,256]{2,1,0:T(8,128)S(1)}, f32[4,16,256]{2,1,0:T(8,128)S(1)}, u32[]{:S(2)}, u32[]{:S(2)}) collective-permute-start(f32[4,16,256]{2,1,0:T(8,128)S(1)} %slice.1311), channel_id=1, source_target_pairs={{0,1},{1,2},{2,3},{3,4},{4,5},{5,6},{6,7},{7,8},{8,9},{9,10},{10,1... | collective-permute-start | bytes 196616 | tf_op jit(solution)/shard_map/ppermute | solution.py:18
  69.2 11.2 %collective-permute-start.4 = (f32[4,16,256]{2,1,0:T(8,128)S(1)}, f32[4,16,256]{2,1,0:T(8,128)S(1)}, u32[]{:S(2)}, u32[]{:S(2)}) collective-permute-start(f32[4,16,256]{2,1,0:T(8,128)S(1)} %slice.1308), channel_id=1, source_target_pairs={{1,0},{2,1},{3,2},{4,3},{5,4},{6,5},{7,6},{8,7},{9,8},{10,9},{11,1... | collective-permute-start | bytes 196616 | tf_op jit(solution)/shard_map/ppermute | solution.py:19
  75.2 12.4 %collective-permute-start.16 = (f32[4,16,256]{2,1,0:T(8,128)S(1)}, f32[4,16,256]{2,1,0:T(8,128)S(1)}, u32[]{:S(2)}, u32[]{:S(2)}) collective-permute-start(f32[4,16,256]{2,1,0:T(8,128)S(1)} %get-tuple-element.40), channel_id=1, source_target_pairs={{1,0},{2,1},{3,2},{4,3},{5,4},{6,5},{7,6},{8,7},{9,8},{10,9},{11,1... | collective-permute-start | bytes 196616 | tf_op jit(solution)/shard_map/ppermute | solution.py:19
  76.5 11.1 %collective-permute-start.17 = (f32[4,16,256]{2,1,0:T(8,128)S(1)}, f32[4,16,256]{2,1,0:T(8,128)S(1)}, u32[]{:S(2)}, u32[]{:S(2)}) collective-permute-start(f32[4,16,256]{2,1,0:T(8,128)S(1)} %get-tuple-element.41), channel_id=1, source_target_pairs={{0,1},{1,2},{2,3},{3,4},{4,5},{5,6},{6,7},{7,8},{8,9},{9,10},{10,1... | collective-permute-start | bytes 196616 | tf_op jit(solution)/shard_map/ppermute | solution.py:18
  82.5 14.7 %collective-permute-start.7 = (f32[4,16,256]{2,1,0:T(8,128)S(1)}, f32[4,16,256]{2,1,0:T(8,128)S(1)}, u32[]{:S(2)}, u32[]{:S(2)}) collective-permute-start(f32[4,16,256]{2,1,0:T(8,128)S(1)} %slice.1340), channel_id=1, source_target_pairs={{0,1},{1,2},{2,3},{3,4},{4,5},{5,6},{6,7},{7,8},{8,9},{9,10},{10,1... | collective-permute-start | bytes 196616 | tf_op jit(solution)/shard_map/ppermute | solution.py:18
  86.3 11.0 %collective-permute-start.6 = (f32[4,16,256]{2,1,0:T(8,128)S(1)}, f32[4,16,256]{2,1,0:T(8,128)S(1)}, u32[]{:S(2)}, u32[]{:S(2)}) collective-permute-start(f32[4,16,256]{2,1,0:T(8,128)S(1)} %slice.1337), channel_id=1, source_target_pairs={{1,0},{2,1},{3,2},{4,3},{5,4},{6,5},{7,6},{8,7},{9,8},{10,9},{11,1... | collective-permute-start | bytes 196616 | tf_op jit(solution)/shard_map/ppermute | solution.py:19
  92.1 13.3 %collective-permute-start.18 = (f32[4,16,256]{2,1,0:T(8,128)S(1)}, f32[4,16,256]{2,1,0:T(8,128)S(1)}, u32[]{:S(2)}, u32[]{:S(2)}) collective-permute-start(f32[4,16,256]{2,1,0:T(8,128)S(1)} %get-tuple-element.38), channel_id=1, source_target_pairs={{1,0},{2,1},{3,2},{4,3},{5,4},{6,5},{7,6},{8,7},{9,8},{10,9},{11,1... | collective-permute-start | bytes 196616 | tf_op jit(solution)/shard_map/ppermute | solution.py:19
  93.4 12.1 %collective-permute-start.19 = (f32[4,16,256]{2,1,0:T(8,128)S(1)}, f32[4,16,256]{2,1,0:T(8,128)S(1)}, u32[]{:S(2)}, u32[]{:S(2)}) collective-permute-start(f32[4,16,256]{2,1,0:T(8,128)S(1)} %get-tuple-element.39), channel_id=1, source_target_pairs={{0,1},{1,2},{2,3},{3,4},{4,5},{5,6},{6,7},{7,8},{8,9},{9,10},{10,1... | collective-permute-start | bytes 196616 | tf_op jit(solution)/shard_map/ppermute | solution.py:18
  99.4 15.6 %collective-permute-start.9 = (f32[4,16,256]{2,1,0:T(8,128)S(1)}, f32[4,16,256]{2,1,0:T(8,128)S(1)}, u32[]{:S(2)}, u32[]{:S(2)}) collective-permute-start(f32[4,16,256]{2,1,0:T(8,128)S(1)} %slice.1369), channel_id=1, source_target_pairs={{0,1},{1,2},{2,3},{3,4},{4,5},{5,6},{6,7},{7,8},{8,9},{9,10},{10,1... | collective-permute-start | bytes 196616 | tf_op jit(solution)/shard_map/ppermute | solution.py:18
  104.1 11.0 %collective-permute-start.8 = (f32[4,16,256]{2,1,0:T(8,128)S(1)}, f32[4,16,256]{2,1,0:T(8,128)S(1)}, u32[]{:S(2)}, u32[]{:S(2)}) collective-permute-start(f32[4,16,256]{2,1,0:T(8,128)S(1)} %slice.1366), channel_id=1, source_target_pairs={{1,0},{2,1},{3,2},{4,3},{5,4},{6,5},{7,6},{8,7},{9,8},{10,9},{11,1... | collective-permute-start | bytes 196616 | tf_op jit(solution)/shard_map/ppermute | solution.py:19
  109.9 13.7 %collective-permute-start.20 = (f32[4,16,256]{2,1,0:T(8,128)S(1)}, f32[4,16,256]{2,1,0:T(8,128)S(1)}, u32[]{:S(2)}, u32[]{:S(2)}) collective-permute-start(f32[4,16,256]{2,1,0:T(8,128)S(1)} %get-tuple-element.36), channel_id=1, source_target_pairs={{1,0},{2,1},{3,2},{4,3},{5,4},{6,5},{7,6},{8,7},{9,8},{10,9},{11,1... | collective-permute-start | bytes 196616 | tf_op jit(solution)/shard_map/ppermute | solution.py:19
  111.2 12.4 %collective-permute-start.21 = (f32[4,16,256]{2,1,0:T(8,128)S(1)}, f32[4,16,256]{2,1,0:T(8,128)S(1)}, u32[]{:S(2)}, u32[]{:S(2)}) collective-permute-start(f32[4,16,256]{2,1,0:T(8,128)S(1)} %get-tuple-element.37), channel_id=1, source_target_pairs={{0,1},{1,2},{2,3},{3,4},{4,5},{5,6},{6,7},{7,8},{8,9},{9,10},{10,1... | collective-permute-start | bytes 196616 | tf_op jit(solution)/shard_map/ppermute | solution.py:18
  117.2 10.7 %collective-permute-start.11 = (f32[4,16,256]{2,1,0:T(8,128)S(1)}, f32[4,16,256]{2,1,0:T(8,128)S(1)}, u32[]{:S(2)}, u32[]{:S(2)}) collective-permute-start(f32[4,16,256]{2,1,0:T(8,128)S(1)} %slice.1398), channel_id=1, source_target_pairs={{0,1},{1,2},{2,3},{3,4},{4,5},{5,6},{6,7},{7,8},{8,9},{9,10},{10,1... | collective-permute-start | bytes 196616 | tf_op jit(solution)/shard_map/ppermute | solution.py:18
  122.0 6.0 %collective-permute-start.10 = (f32[4,16,256]{2,1,0:T(8,128)S(1)}, f32[4,16,256]{2,1,0:T(8,128)S(1)}, u32[]{:S(2)}, u32[]{:S(2)}) collective-permute-start(f32[4,16,256]{2,1,0:T(8,128)S(1)} %slice.1395), channel_id=1, source_target_pairs={{1,0},{2,1},{3,2},{4,3},{5,4},{6,5},{7,6},{8,7},{9,8},{10,9},{11,1... | collective-permute-start | bytes 196616 | tf_op jit(solution)/shard_map/ppermute | solution.py:19
  (7 other events, 5.0 us)
where the time goes:
time: 186 us; the launch traced here: 185 us
  starting transfers between devices  70.5 us (38%)
  blocking collectives  50.9 us (27%)
  other arithmetic  40 us (22%)
  local copies, waits for them, and re-layouts  12.8 us (7%)
  waiting for transfers between devices  6.3 us (3%)
  between operations  4.54 us (2%)
    psum x1, blocking collectives, body(): lax.psum((jnp.sum(halves[0] * halves[0]), jnp.sum(halves[1] * halves[1]))...  43.4 us
    ppermute x11, starting transfers between devices, padded(): before = lax.ppermute(last, axis, up)  40.5 us
    scatter-add x13, other arithmetic, inject(): return flattened.at[positions].add(amounts).reshape(wave_field.shape)  27.9 us
    ppermute x11, starting transfers between devices, padded(): after = lax.ppermute(initial, axis, down)  14.6 us
    all_to_all x1, starting transfers between devices, body(): lax.all_to_all(sent_values, 'space', split_axis=0, concat_axis=0, tiled=T...  7.98 us
    all_to_all x1, blocking collectives, body(): lax.all_to_all(gradient[None], 'batch', split_axis=2, concat_axis=0, tile...  7.5 us
    all_to_all x1, starting transfers between devices, body(): lax.all_to_all(sent_cells, 'space', split_axis=0, concat_axis=0, tiled=True)  7.39 us
    all_to_all x1, waiting for transfers between devices, body(): lax.all_to_all(sent_values, 'space', split_axis=0, concat_axis=0, tiled=T...  6.24 us
  transfers between devices with their start and end apart: 24, of which 1 were waited for; matrix products, arithmetic and copies ran while one was open for 23% of the time, Pallas kernels for 0%

commit v1 on v0

v1 whole, which is shorter than its diff:
```python
import functools
import jax
import jax.numpy as jnp
from jax import lax
from jax.experimental import pallas as pl
from jax.experimental.pallas import tpu as pltpu
from jax.sharding import PartitionSpec as P

center_tap = -205.0 / 72.0
stencil_taps = (1.6, -0.2, 8.0 / 315.0, -1.0 / 560.0)
epsilon = 1e-06
MESH = pl.DeviceIdType.MESH
F32, BF16, I32 = jnp.float32, jnp.bfloat16, jnp.int32
REACH = 3
HOPS = (-1, 1, -2, 2, -3, 3)


def halves_of(x):
    high = x.astype(BF16)
    return high, (x - high.astype(F32)).astype(BF16)


def dot(a, b):
    return lax.dot_general(a, b, (((1,), (0,)), ((), ())), preferred_element_type=F32)


def dot_lanes(a, b):
    return lax.dot_general(a, b, (((1,), (1,)), ((), ())), preferred_element_type=F32)


def taps_at(distance, middle):
    value = jnp.where(distance == 0, middle, 0.0)
    for k in range(4):
        value = jnp.where(distance == k + 1, stencil_taps[k], value)
    return value


def placed(row_ids, high, low, onehot, first, count):
    rows = lax.broadcasted_iota(I32, (count, row_ids.shape[1]), 0) + first
    here = rows == row_ids
    stacked = jnp.concatenate([jnp.where(here, high, 0.0), jnp.where(here, low, 0.0)], axis=0)
    both = dot_lanes(stacked.astype(BF16), onehot)
    return both[:count] + both[count:]


def kernel(
    parties, batches, steps, block, width_y, width_z, cap, rows,
    cour, wav, s_own, s_cell, tra, t_own, t_cell,
    upd, agr,
    vbuf, sbuf, rbuf, relay, cext, field_r, ua, ub, uh, ul, aa, ab, ah, al, dbuf,
    taps_xy, taps_z, gbuf, gin, nbuf,
    a2a_s, a2a_r, c_s, c_r, l_s, l_r, g_s, g_r, n_s, n_r,
):
    b = lax.axis_index("batch")
    me = lax.axis_index("space")
    total = parties * batches
    mine = b * parties + me
    shift = width_y * 4
    tiles = 2 * REACH + 1

    barrier = pltpu.get_barrier_semaphore()

    def greet(k, carry):
        other = lax.rem(mine + k, total)
        pl.semaphore_signal(
            barrier, inc=1, device_id=(other // parties, lax.rem(other, parties)), device_id_type=MESH
        )
        return carry

    lax.fori_loop(1, total, greet, 0)

    vbuf[0:steps, :] = tra[...]
    vbuf[steps : steps + 1, :] = t_cell[...].astype(F32)
    owners = t_own[...]
    match = (lax.broadcasted_iota(I32, (parties, rows), 0) == owners).astype(F32)
    before = lax.broadcasted_iota(I32, (rows, rows), 0) < lax.broadcasted_iota(I32, (rows, rows), 1)
    ahead = dot(match.astype(BF16), before.astype(F32).astype(BF16))
    rank = jnp.sum(match * ahead, axis=0, keepdims=True)
    slot = owners * cap + rank.astype(I32)
    slots = parties * cap
    chosen = (lax.broadcasted_iota(I32, (slots, rows), 0) == slot).astype(F32).astype(BF16)
    values = vbuf[...]
    v_high = values.astype(BF16).astype(F32)
    pieces = jnp.concatenate([v_high, values - v_high], axis=0).astype(BF16)
    sorted_two = dot_lanes(pieces, chosen)
    ordered = sorted_two[:8] + sorted_two[8:]
    group = 128 // cap
    spot = lax.rem(me, group)
    lanes = lax.broadcasted_iota(I32, (8, 128), 1)
    keep = (lanes // cap) == spot
    for dest in range(parties):
        four = ordered[:, (dest // group) * 128 : (dest // group) * 128 + 128]
        turned = pltpu.roll(four, lax.rem(spot - dest % group + group, group) * cap, 1)
        sbuf[dest] = jnp.where(keep, turned, 0.0)
    rbuf[me] = sbuf[me]

    pl.semaphore_wait(barrier, total - 1)

    def route(k):
        dest = lax.rem(me + k, parties)
        return pltpu.make_async_remote_copy(
            src_ref=sbuf.at[dest], dst_ref=rbuf.at[me], send_sem=a2a_s.at[dest],
            recv_sem=a2a_r.at[me], device_id=(b, dest), device_id_type=MESH,
        )

    def arrive(k):
        origin = lax.rem(me + k, parties)
        return pltpu.make_async_remote_copy(
            src_ref=sbuf.at[origin], dst_ref=rbuf.at[origin], send_sem=a2a_s.at[origin],
            recv_sem=a2a_r.at[origin], device_id=(b, origin), device_id_type=MESH,
        )

    def start_route(k, carry):
        route(k).start()
        return carry

    lax.fori_loop(1, parties, start_route, 0)

    def cour_copy(n, hop, receiving):
        part = block
        lo = 0
        if abs(hop) == REACH:
            part = block // 2
            lo = block // 2 if hop > 0 else 0
        at = REACH - hop
        return pltpu.make_async_remote_copy(
            src_ref=cour.at[pl.ds(lo, part)], dst_ref=cext.at[pl.ds(at * block + lo, part)],
            send_sem=c_s.at[n], recv_sem=c_r.at[at],
            device_id=(b, me - hop if receiving else me + hop), device_id_type=MESH,
        )

    def relay_copy(n, hop, receiving):
        at = REACH - hop
        return pltpu.make_async_remote_copy(
            src_ref=relay.at[REACH], dst_ref=relay.at[at], send_sem=l_s.at[n],
            recv_sem=l_r.at[at], device_id=(b, me - hop if receiving else me + hop),
            device_id_type=MESH,
        )

    def inside(place):
        return (place >= 0) & (place < parties)

    for n, hop in enumerate(HOPS):
        @pl.when(inside(me + hop))
        def _():
            cour_copy(n, hop, False).start()

        at = REACH - hop

        @pl.when(jnp.logical_not(inside(me - hop)))
        def _():
            cext[pl.ds(at * block, block), :] = jnp.zeros((block, width_z), F32)
            relay[at] = jnp.zeros(relay.shape[1:], F32)

    cext[pl.ds(REACH * block, block), :] = cour[...]

    i = lax.broadcasted_iota(I32, (block, 2 * block), 0)
    j = lax.broadcasted_iota(I32, (block, 2 * block), 1)
    xi, yi = i // width_y, lax.rem(i, width_y)
    xj, yj = j // width_y - 4, lax.rem(j, width_y)
    along_x = jnp.where(yi == yj, taps_at(jnp.abs(xi - xj), 3.0 * center_tap), 0.0)
    along_y = jnp.where(xi == xj, taps_at(jnp.abs(yi - yj), 0.0), 0.0)
    taps_xy[0], taps_xy[1] = halves_of(along_x + along_y)
    zi = lax.broadcasted_iota(I32, (width_z, width_z), 0)
    zj = lax.broadcasted_iota(I32, (width_z, width_z), 1)
    taps_z[0], taps_z[1] = halves_of(taps_at(jnp.abs(zi - zj), 0.0))

    sources = s_own.shape[1]
    source_row = (s_own[...] - me + REACH) * block + s_cell[...] // width_z
    source_hot = (
        lax.broadcasted_iota(I32, (width_z, sources), 0) == lax.rem(s_cell[...], width_z)
    ).astype(F32).astype(BF16)
    wave = wav[...]
    wave_high = wave.astype(BF16).astype(F32)
    wave_low = wave - wave_high

    def sources_at(t, first, count):
        return placed(
            source_row, wave_high[t : t + 1], wave_low[t : t + 1], source_hot, first, count
        )

    for tile in range(tiles):
        r = pl.ds(tile * block, block)
        start = sources_at(0, tile * block, block)
        ua[r, :] = start
        uh[0, r, :], ul[0, r, :] = halves_of(start)

    def end_arrive(k, carry):
        arrive(k).wait_recv()
        return carry

    lax.fori_loop(1, parties, end_arrive, 0)
    for q in range(slots // 128):
        gathered = rbuf[q * group]
        for s in range(1, group):
            gathered = gathered + rbuf[q * group + s]
        relay[REACH, :, q * 128 : q * 128 + 128] = gathered
    for n, hop in enumerate(HOPS):
        @pl.when(inside(me + hop))
        def _():
            relay_copy(n, hop, False).start()

    last = steps - 1

    def stations(at):
        got = relay[at]
        cell = got[7:8].astype(I32)
        row, column = cell // width_z, lax.rem(cell, width_z)
        hot = (lax.broadcasted_iota(I32, (width_z, slots), 0) == column).astype(F32).astype(BF16)
        high = got.astype(BF16).astype(F32)
        low = got - high
        for t in range(1, steps):
            needed = -(-(t - 1) * 4 // 8)
            if abs(at - REACH) <= needed:
                field_r[t, pl.ds(at * block, block), :] = placed(
                    row, high[t : t + 1], low[t : t + 1], hot, 0, block
                )

    stations(REACH)
    for n, hop in enumerate(HOPS):
        @pl.when(inside(me - hop))
        def _():
            relay_copy(n, hop, True).wait_recv()

        stations(REACH - hop)
    for n, hop in enumerate(HOPS):
        @pl.when(inside(me - hop))
        def _():
            cour_copy(n, hop, True).wait_recv()

    xy_high, xy_low = taps_xy[0], taps_xy[1]
    z_high, z_low = taps_z[0], taps_z[1]

    def laplace(high, low, slot_at, first):
        wide = pl.ds(first - shift, 2 * block)
        own = pl.ds(first, block)
        h, l = high[slot_at, wide, :], low[slot_at, wide, :]
        ho, lo = high[slot_at, own, :], low[slot_at, own, :]
        out = dot(xy_high, h) + dot(xy_low, h) + dot(xy_high, l)
        return out + dot(ho, z_high) + dot(ho, z_low) + dot(lo, z_high)

    for tile in range(2 * tiles - 2):
        r = pl.ds(shift + tile * shift, shift)
        first_b = cext[r, :] * field_r[last, r, :]
        ah[0, r, :], al[0, r, :] = halves_of(first_b)

    fields = (ua, ub)
    adjoints = (aa, ab)
    own = pl.ds(REACH * block, block)
    gradient = None
    for t in range(1, steps):
        now, later = (t - 1) % 2, t % 2
        for tile in range(steps - t):
            first = shift * t + block * tile
            r = pl.ds(first, block)
            change = cext[r, :] * laplace(uh, ul, now, first) + sources_at(t, first, block)
            if first == REACH * block:
                dbuf[t] = change
            elif t % 2 == 1 and abs(first - REACH * block) == shift:
                half = block // 2
                if first < REACH * block:
                    dbuf[t, :half, :] = change[half:]
                else:
                    dbuf[t, half:, :] = change[:half]
            if t < last:
                following = 2.0 * fields[now][r, :] + change
                if t > 1:
                    following = following - fields[later][r, :]
                fields[later][r, :] = following
                uh[later, r, :], ul[later, r, :] = halves_of(following)
        s = last - t
        if s >= 1:
            for tile in range(s):
                first = shift * (steps - s) + block * tile
                r = pl.ds(first, block)
                newer = laplace(ah, al, now, first) + field_r[s, r, :]
                if t == 1:
                    newer = newer + 2.0 * field_r[last, r, :]
                elif t == 2:
                    newer = newer + 2.0 * adjoints[now][r, :] - field_r[last, r, :]
                else:
                    newer = newer + 2.0 * adjoints[now][r, :] - adjoints[later][r, :]
                adjoints[later][r, :] = newer
                if s > 1:
                    ah[later, r, :], al[later, r, :] = halves_of(cext[r, :] * newer)
            field_r[s, own, :] = adjoints[later][own, :]
    for t in range(1, steps):
        term = field_r[t, own, :] * dbuf[t]
        gradient = term if gradient is None else gradient + term

    cells_x = block // width_y
    half_y = width_y // 2
    shaped = gradient.reshape(cells_x, 2, half_y, width_z)
    gbuf[0] = shaped[:, 0]
    gbuf[1] = shaped[:, 1]
    swap = pltpu.make_async_remote_copy(
        src_ref=gbuf.at[1 - b], dst_ref=gin, send_sem=g_s, recv_sem=g_r,
        device_id=(1 - b, me), device_id_type=MESH,
    )
    squares = jnp.sum(gradient * gradient, axis=0, keepdims=True)
    nbuf[mine] = squares[:, :128] + squares[:, 128:]

    def norm_out(k):
        other = lax.rem(mine + k, total)
        return pltpu.make_async_remote_copy(
            src_ref=nbuf.at[mine], dst_ref=nbuf.at[mine], send_sem=n_s.at[other],
            recv_sem=n_r.at[mine], device_id=(other // parties, lax.rem(other, parties)),
            device_id_type=MESH,
        )

    def norm_in(k):
        other = lax.rem(mine + k, total)
        return pltpu.make_async_remote_copy(
            src_ref=nbuf.at[mine], dst_ref=nbuf.at[other], send_sem=n_s.at[other],
            recv_sem=n_r.at[other], device_id=(other // parties, lax.rem(other, parties)),
            device_id_type=MESH,
        )

    def start_norm(k, carry):
        norm_out(k).start()
        return carry

    def end_norm(k, carry):
        norm_in(k).wait_recv()
        return carry

    lax.fori_loop(1, total, start_norm, 0)
    swap.start()

    def end_route(k, carry):
        route(k).wait_send()
        return carry

    lax.fori_loop(1, parties, end_route, 0)
    for n, hop in enumerate(HOPS):
        @pl.when(inside(me + hop))
        def _():
            cour_copy(n, hop, False).wait_send()
            relay_copy(n, hop, False).wait_send()

    lax.fori_loop(1, total, end_norm, 0)
    cells = float(block * width_z * parties)
    mean_first = jnp.sum(jnp.sum(nbuf[0:parties], axis=0), axis=1, keepdims=True) / cells
    mean_second = jnp.sum(jnp.sum(nbuf[parties:total], axis=0), axis=1, keepdims=True) / cells
    scale = 1.0 / jnp.sqrt((mean_first + mean_second) / 2.0 + epsilon)
    agr[...] = jnp.broadcast_to(
        (mean_first + epsilon) / (mean_first + mean_second + 2.0 * epsilon), agr.shape
    )
    swap.wait()
    upd[...] = (gbuf[b] + gin[...]) * scale.reshape(1, 1, 1)

    def end_norm_sent(k, carry):
        norm_out(k).wait_send()
        return carry

    lax.fori_loop(1, total, end_norm_sent, 0)


def body(courant, wavelet, source_owner, source_cell, traces, station_owner, station_cell):
    width_x, width_y, width_z = courant.shape
    rows, steps = traces.shape[1:]
    parties, batches = lax.axis_size("space"), lax.axis_size("batch")
    block = width_x * width_y
    cap = max(2 * rows // parties, 4)
    window = (2 * REACH + 1) * block
    vmem = pl.BlockSpec(memory_space=pltpu.VMEM)
    dma = pltpu.SemaphoreType.DMA
    update, agreement = pl.pallas_call(
        functools.partial(kernel, parties, batches, steps, block, width_y, width_z, cap, rows),
        out_shape=(
            jax.ShapeDtypeStruct((width_x, width_y // 2, width_z), F32),
            jax.ShapeDtypeStruct((1, 128), F32),
        ),
        in_specs=[vmem] * 7,
        out_specs=(vmem, vmem),
        scratch_shapes=[
            pltpu.VMEM((8, rows), F32),
            pltpu.VMEM((parties, 8, 128), F32),
            pltpu.VMEM((parties, 8, 128), F32),
            pltpu.VMEM((2 * REACH + 1, 8, parties * cap), F32),
            pltpu.VMEM((window, width_z), F32),
            pltpu.VMEM((steps, window, width_z), F32),
            pltpu.VMEM((window, width_z), F32),
            pltpu.VMEM((window, width_z), F32),
            pltpu.VMEM((2, window, width_z), BF16),
            pltpu.VMEM((2, window, width_z), BF16),
            pltpu.VMEM((window, width_z), F32),
            pltpu.VMEM((window, width_z), F32),
            pltpu.VMEM((2, window, width_z), BF16),
            pltpu.VMEM((2, window, width_z), BF16),
            pltpu.VMEM((steps, block, width_z), F32),
            pltpu.VMEM((2, block, 2 * block), BF16),
            pltpu.VMEM((2, width_z, width_z), BF16),
            pltpu.VMEM((2, width_x, width_y // 2, width_z), F32),
            pltpu.VMEM((width_x, width_y // 2, width_z), F32),
            pltpu.VMEM((parties * batches, 1, 128), F32),
            dma((parties,)), dma((parties,)),
            dma((6,)), dma((7,)), dma((6,)), dma((7,)),
            dma, dma,
            dma((parties * batches,)), dma((parties * batches,)),
        ],
        compiler_params=pltpu.CompilerParams(
            collective_id=0, has_side_effects=True, vmem_limit_bytes=40 * 1024 * 1024
        ),
    )(
        courant.reshape(block, width_z),
        wavelet[0].T,
        source_owner,
        source_cell,
        traces[0].T,
        station_owner.reshape(1, rows),
        station_cell,
    )
    return update, agreement[0, :1]


def solution(mesh):
    return jax.shard_map(
        body,
        mesh=mesh,
        in_specs=(
            P("space", None, None),
            P("batch", None, None),
            P("batch", None),
            P("batch", None),
            P("batch", "space", None),
            P("batch", "space", None),
            P("batch", "space"),
        ),
        out_specs=(P("space", "batch", None), P()),
        check_vma=False,
    )
```

time: 186 us -> 37.9 us (0.20)
  starting transfers between devices: 70.5 us -> 0 us
  blocking collectives: 50.9 us -> 0 us
  other arithmetic: 40 us -> 0 us
  Pallas kernels: 0 us -> 32.9 us
  local copies, waits for them, and re-layouts: 12.8 us -> 2.93 us
  waiting for transfers between devices: 6.3 us -> 0 us
  between operations: 4.54 us -> 1.84 us
    ppermute x22 -> x0, starting transfers between devices: 55.1 us -> none  [the longest x11 40.5 us: padded(): before = lax.ppermute(last, axis, up)]
    psum x1 -> x0, blocking collectives: 43.4 us -> none  [body(): lax.psum((jnp.sum(halves[0] * halves[0]), jnp.sum(halves[1] * halves[1]))...]
    pallas_call x0 -> x1, Pallas kernels: none -> 32.9 us  [body(): pl.pallas_call(functools.partial(kernel, parties, batches, steps, block,...]
    scatter-add x13 -> x0, other arithmetic: 27.9 us -> none  [inject(): return flattened.at[positions].add(amounts).reshape(wave_field.shape)]
    all_to_all x2 -> x0, starting transfers between devices: 15.4 us -> none  [the longest x1 7.98 us: body(): lax.all_to_all(sent_values, 'space', split_axis=0, concat_axis=0, tiled=T...]
    all_to_all x1 -> x0, blocking collectives: 7.5 us -> none  [body(): lax.all_to_all(gradient[None], 'batch', split_axis=2, concat_axis=0, tile...]
    add x12 -> x0, other arithmetic: 6.63 us -> none  [the longest x6 3.5 us: body(): 2.0 * current - snapshots[moment - 1] + courant * stencil(current)]
    all_to_all x2 -> x0, waiting for transfers between devices: 6.24 us -> none  [the longest x1 6.24 us: body(): lax.all_to_all(sent_values, 'space', split_axis=0, concat_axis=0, tiled=T...]
  transfers between devices with their start and end apart: 24 -> 0, of which waited for: 1 -> 0; matrix products, arithmetic and copies ran while one was open for 23% -> 0% of each run, Pallas kernels for 0% -> 0%
where the time goes in v1:
time: 37.9 us; the launch traced here: 37.6 us
  Pallas kernels  32.9 us (87%)
  local copies, waits for them, and re-layouts  2.93 us (8%)
  between operations  1.84 us (5%)
    pallas_call x1, Pallas kernels, body(): pl.pallas_call(functools.partial(kernel, parties, batches, steps, block,...  32.9 us
    unnamed x15, local copies, waits for them, and re-layouts  2.93 us

profile of v1, /device:TPU:0, one launch (start us, length us, event | category | flops | bytes accessed | tf_op | source)
XLA Modules:
  0.0 37.6 jit_solution(11908322936002306514)
XLA Ops:
  0.6 0.0 copy-start.5
  0.6 0.7 %copy.14 = f32[1,64,7]{1,2,0:T(8,128)S(1)} copy(f32[1,64,7]{1,0,2:T(1,128)} %param.8) | data formatting | bytes 3584
  1.3 0.0 copy-done.5
  1.3 0.0 copy-start.2
  1.3 0.0 copy-start.4
  1.3 0.0 copy-start.1
  1.4 0.0 copy-start.3
  1.4 0.6 %copy-done.2 = s32[1,256]{1,0:T(1,128)S(1)} copy-done((s32[1,256]{1,0:T(1,128)S(1)}, s32[1,256]{1,0:T(1,128)}, u32[]{:S(2)}) %copy-start.2) | copy-done | bytes 1048
  2.0 0.0 copy-done.4
  2.0 0.0 copy-done.1
  2.0 0.0 copy-done.3
  2.0 0.0 copy-start
  2.1 0.9 %copy-done = f32[8,16,256]{2,1,0:T(8,128)S(1)} copy-done((f32[8,16,256]{2,1,0:T(8,128)S(1)}, f32[8,16,256]{2,1,0:T(8,128)}, u32[]{:S(2)}) %copy-start) | copy-done | bytes 131096
  3.0 32.9 %shard_map.86 = (f32[8,8,256]{2,1,0:T(8,128)S(1)}, f32[1,128]{1,0:T(1,128)S(1)}) custom-call(f32[128,256]{1,0:T(8,128)S(1)} %bitcast.14, f32[7,64]{1,0:T(8,128)S(1)} %bitcast.16, s32[1,64]{1,0:T(1,128)S(1)} %copy-done.3, s32[1,64]{1,0:T(1,128)S(1)} %copy-done.4, f32[7,256]{1,0:T(8,128)S(1)} %bitcast.15, s32[1,256]{1,0:T(1,128)S(1)} %bitcast.17, ...), custom_call_target="tpu_custom_call" | custom-call | tf_op jit(solution)/shard_map/pallas_call | solution.py:368
  35.9 0.6 %copy.17 = f32[8,8,256]{2,1,0:T(8,128)} copy(f32[8,8,256]{2,1,0:T(8,128)S(1)} %get-tuple-element.8) | data formatting | bytes 131072
  (1 shorter events, 0.0 us)
Async XLA Ops:
  0.6 0.7 %copy-start.5 = (f32[1,256,7]{1,0,2:T(1,128)S(1)}, f32[1,256,7]{1,0,2:T(1,128)}, u32[]{:S(2)}) copy-start(f32[1,256,7]{1,0,2:T(1,128)} %param.11) | copy-start | bytes 21508
  1.3 0.7 %copy-start.2 = (s32[1,256]{1,0:T(1,128)S(1)}, s32[1,256]{1,0:T(1,128)}, u32[]{:S(2)}) copy-start(s32[1,256]{1,0:T(1,128)} %t_cell.1) | copy-start | bytes 3076
  1.3 0.7 %copy-start.4 = (s32[1,64]{1,0:T(1,128)S(1)}, s32[1,64]{1,0:T(1,128)}, u32[]{:S(2)}) copy-start(s32[1,64]{1,0:T(1,128)} %s_cell.1) | copy-start | bytes 772
  1.3 0.7 %copy-start.1 = (s32[1,256,1]{1,2,0:T(1,128)S(1)}, s32[1,256,1]{1,2,0:T(1,128)}, u32[]{:S(2)}) copy-start(s32[1,256,1]{1,2,0:T(1,128)} %param.12) | copy-start | bytes 3076
  1.4 0.7 %copy-start.3 = (s32[1,64]{1,0:T(1,128)S(1)}, s32[1,64]{1,0:T(1,128)}, u32[]{:S(2)}) copy-start(s32[1,64]{1,0:T(1,128)} %s_own.1) | copy-start | bytes 772
  2.0 0.9 %copy-start = (f32[8,16,256]{2,1,0:T(8,128)S(1)}, f32[8,16,256]{2,1,0:T(8,128)}, u32[]{:S(2)}) copy-start(f32[8,16,256]{2,1,0:T(8,128)} %param.7) | copy-start | bytes 393220

commit v2 on v1

--- a/solution.py
+++ b/solution.py
@@ -6,8 +6,9 @@
 from jax.experimental.pallas import tpu as pltpu
 from jax.sharding import PartitionSpec as P
 
-center_tap = -205.0 / 72.0
-stencil_taps = (1.6, -0.2, 8.0 / 315.0, -1.0 / 560.0)
+unit = 5040.0
+stencil_taps = (8064.0, -1008.0, 128.0, -9.0)
+middle_xy, middle_z = -43008.0, -42.0
 epsilon = 1e-06
 MESH = pl.DeviceIdType.MESH
 F32, BF16, I32 = jnp.float32, jnp.bfloat16, jnp.int32
@@ -35,18 +36,20 @@
     return value
 
 
-def placed(row_ids, high, low, onehot, first, count):
+def placed(row_ids, amounts, onehot, first, count):
     rows = lax.broadcasted_iota(I32, (count, row_ids.shape[1]), 0) + first
     here = rows == row_ids
-    stacked = jnp.concatenate([jnp.where(here, high, 0.0), jnp.where(here, low, 0.0)], axis=0)
-    both = dot_lanes(stacked.astype(BF16), onehot)
-    return both[:count] + both[count:]
+    stacked = [jnp.where(here, part, 0.0).astype(BF16) for pair in amounts for part in pair]
+    both = dot_lanes(jnp.concatenate(stacked, axis=0), onehot)
+    both = both.reshape(len(amounts), 2, count, both.shape[1])
+    return [both[k, 0] + both[k, 1] for k in range(len(amounts))]
 
 
 def kernel(
     parties, batches, steps, block, width_y, width_z, cap, rows,
-    cour, wav, s_own, s_cell, tra, t_own, t_cell,
+    cour_in, wav_in, s_own_in, s_cell_in, tra_in, t_own_in, t_cell_in,
     upd, agr,
+    cour, wav, s_own, s_cell, tra, t_own, t_cell, in_s,
     vbuf, sbuf, rbuf, relay, cext, field_r, ua, ub, uh, ul, aa, ab, ah, al, dbuf,
     taps_xy, taps_z, gbuf, gin, nbuf,
     a2a_s, a2a_r, c_s, c_r, l_s, l_r, g_s, g_r, n_s, n_r,
@@ -58,18 +61,29 @@
     shift = width_y * 4
     tiles = 2 * REACH + 1
 
+    pairs = (
+        (t_own_in, t_own), (t_cell_in, t_cell), (tra_in, tra), (cour_in, cour),
+        (wav_in, wav), (s_own_in, s_own), (s_cell_in, s_cell),
+    )
+    loads = [pltpu.make_async_copy(a, c, in_s.at[k]) for k, (a, c) in enumerate(pairs)]
+    for load in loads:
+        load.start()
+
     barrier = pltpu.get_barrier_semaphore()
 
     def greet(k, carry):
         other = lax.rem(mine + k, total)
         pl.semaphore_signal(
-            barrier, inc=1, device_id=(other // parties, lax.rem(other, parties)), device_id_type=MESH
+            barrier, inc=1, device_id=(lax.div(other, parties), lax.rem(other, parties)), device_id_type=MESH
         )
         return carry
 
     lax.fori_loop(1, total, greet, 0)
 
-    vbuf[0:steps, :] = tra[...]
+    for load in loads:
+        load.wait()
+    for t in range(steps):
+        vbuf[t : t + 1, :] = tra[t]
     vbuf[steps : steps + 1, :] = t_cell[...].astype(F32)
     owners = t_own[...]
     match = (lax.broadcasted_iota(I32, (parties, rows), 0) == owners).astype(F32)
@@ -93,6 +107,8 @@
         turned = pltpu.roll(four, lax.rem(spot - dest % group + group, group) * cap, 1)
         sbuf[dest] = jnp.where(keep, turned, 0.0)
     rbuf[me] = sbuf[me]
+    middle = REACH * block
+    cext[pl.ds(middle, block), :] = cour[...] * (1.0 / unit)
 
     pl.semaphore_wait(barrier, total - 1)
 
@@ -124,7 +140,7 @@
             lo = block // 2 if hop > 0 else 0
         at = REACH - hop
         return pltpu.make_async_remote_copy(
-            src_ref=cour.at[pl.ds(lo, part)], dst_ref=cext.at[pl.ds(at * block + lo, part)],
+            src_ref=cext.at[pl.ds(middle + lo, part)], dst_ref=cext.at[pl.ds(at * block + lo, part)],
             send_sem=c_s.at[n], recv_sem=c_r.at[at],
             device_id=(b, me - hop if receiving else me + hop), device_id_type=MESH,
         )
@@ -152,32 +168,28 @@
             cext[pl.ds(at * block, block), :] = jnp.zeros((block, width_z), F32)
             relay[at] = jnp.zeros(relay.shape[1:], F32)
 
-    cext[pl.ds(REACH * block, block), :] = cour[...]
-
     i = lax.broadcasted_iota(I32, (block, 2 * block), 0)
     j = lax.broadcasted_iota(I32, (block, 2 * block), 1)
     xi, yi = i // width_y, lax.rem(i, width_y)
     xj, yj = j // width_y - 4, lax.rem(j, width_y)
-    along_x = jnp.where(yi == yj, taps_at(jnp.abs(xi - xj), 3.0 * center_tap), 0.0)
+    along_x = jnp.where(yi == yj, taps_at(jnp.abs(xi - xj), middle_xy), 0.0)
     along_y = jnp.where(xi == xj, taps_at(jnp.abs(yi - yj), 0.0), 0.0)
-    taps_xy[0], taps_xy[1] = halves_of(along_x + along_y)
+    taps_xy[...] = (along_x + along_y).astype(BF16)
     zi = lax.broadcasted_iota(I32, (width_z, width_z), 0)
     zj = lax.broadcasted_iota(I32, (width_z, width_z), 1)
-    taps_z[0], taps_z[1] = halves_of(taps_at(jnp.abs(zi - zj), 0.0))
+    taps_z[...] = taps_at(jnp.abs(zi - zj), middle_z).astype(BF16)
 
     sources = s_own.shape[1]
     source_row = (s_own[...] - me + REACH) * block + s_cell[...] // width_z
     source_hot = (
         lax.broadcasted_iota(I32, (width_z, sources), 0) == lax.rem(s_cell[...], width_z)
     ).astype(F32).astype(BF16)
-    wave = wav[...]
-    wave_high = wave.astype(BF16).astype(F32)
-    wave_low = wave - wave_high
-
     def sources_at(t, first, count):
+        wave = wav[t]
+        wave_high = wave.astype(BF16).astype(F32)
         return placed(
-            source_row, wave_high[t : t + 1], wave_low[t : t + 1], source_hot, first, count
-        )
+            source_row, [(wave_high, wave - wave_high)], source_hot, first, count
+        )[0]
 
     for tile in range(tiles):
         r = pl.ds(tile * block, block)
@@ -209,12 +221,10 @@
         hot = (lax.broadcasted_iota(I32, (width_z, slots), 0) == column).astype(F32).astype(BF16)
         high = got.astype(BF16).astype(F32)
         low = got - high
-        for t in range(1, steps):
-            needed = -(-(t - 1) * 4 // 8)
-            if abs(at - REACH) <= needed:
-                field_r[t, pl.ds(at * block, block), :] = placed(
-                    row, high[t : t + 1], low[t : t + 1], hot, 0, block
-                )
+        times = [t for t in range(1, steps) if abs(at - REACH) <= -(-(t - 1) * 4 // 8)]
+        amounts = [(high[t : t + 1], low[t : t + 1]) for t in times]
+        for t, field in zip(times, placed(row, amounts, hot, 0, block)):
+            field_r[t, pl.ds(at * block, block), :] = field
 
     stations(REACH)
     for n, hop in enumerate(HOPS):
@@ -223,26 +233,23 @@
             relay_copy(n, hop, True).wait_recv()
 
         stations(REACH - hop)
-    for n, hop in enumerate(HOPS):
-        @pl.when(inside(me - hop))
-        def _():
-            cour_copy(n, hop, True).wait_recv()
-
-    xy_high, xy_low = taps_xy[0], taps_xy[1]
-    z_high, z_low = taps_z[0], taps_z[1]
+
+    def wait_cour(distance):
+        for n, hop in enumerate(HOPS):
+            if abs(hop) == distance:
+                @pl.when(inside(me - hop))
+                def _():
+                    cour_copy(n, hop, True).wait_recv()
+
+    xy, z = taps_xy[...], taps_z[...]
+
+    def along_z(high, low, slot_at, first, count):
+        r = pl.ds(first, count)
+        return dot(high[slot_at, r, :], z) + dot(low[slot_at, r, :], z)
 
     def laplace(high, low, slot_at, first):
         wide = pl.ds(first - shift, 2 * block)
-        own = pl.ds(first, block)
-        h, l = high[slot_at, wide, :], low[slot_at, wide, :]
-        ho, lo = high[slot_at, own, :], low[slot_at, own, :]
-        out = dot(xy_high, h) + dot(xy_low, h) + dot(xy_high, l)
-        return out + dot(ho, z_high) + dot(ho, z_low) + dot(lo, z_high)
-
-    for tile in range(2 * tiles - 2):
-        r = pl.ds(shift + tile * shift, shift)
-        first_b = cext[r, :] * field_r[last, r, :]
-        ah[0, r, :], al[0, r, :] = halves_of(first_b)
+        return dot(xy, high[slot_at, wide, :]) + dot(xy, low[slot_at, wide, :])
 
     fields = (ua, ub)
     adjoints = (aa, ab)
@@ -250,10 +257,18 @@
     gradient = None
     for t in range(1, steps):
         now, later = (t - 1) % 2, t % 2
-        for tile in range(steps - t):
-            first = shift * t + block * tile
+        start = shift * t
+        z_part = along_z(uh, ul, now, start, block * (steps - t))
+        order = list(range(steps - t))
+        if t == 1:
+            order = sorted(order, key=lambda k: abs(2 * k - steps + t + 1))
+        for place, tile in enumerate(order):
+            if t == 1 and place % 2 == 0:
+                wait_cour(place // 2 + 1)
+            first = start + block * tile
             r = pl.ds(first, block)
-            change = cext[r, :] * laplace(uh, ul, now, first) + sources_at(t, first, block)
+            both = laplace(uh, ul, now, first) + z_part[block * tile : block * tile + block]
+            change = cext[r, :] * both + sources_at(t, first, block)
             if first == REACH * block:
                 dbuf[t] = change
             elif t % 2 == 1 and abs(first - REACH * block) == shift:
@@ -268,12 +283,20 @@
                     following = following - fields[later][r, :]
                 fields[later][r, :] = following
                 uh[later, r, :], ul[later, r, :] = halves_of(following)
+        if t == 1:
+            for tile in range(2 * tiles - 2):
+                r = pl.ds(shift + tile * shift, shift)
+                first_b = cext[r, :] * field_r[last, r, :]
+                ah[0, r, :], al[0, r, :] = halves_of(first_b)
         s = last - t
         if s >= 1:
+            start = shift * (steps - s)
+            z_part = along_z(ah, al, now, start, block * s)
             for tile in range(s):
-                first = shift * (steps - s) + block * tile
+                first = start + block * tile
                 r = pl.ds(first, block)
-                newer = laplace(ah, al, now, first) + field_r[s, r, :]
+                newer = laplace(ah, al, now, first) + z_part[block * tile : block * tile + block]
+                newer = newer + field_r[s, r, :]
                 if t == 1:
                     newer = newer + 2.0 * field_r[last, r, :]
                 elif t == 2:
@@ -304,7 +327,7 @@
         other = lax.rem(mine + k, total)
         return pltpu.make_async_remote_copy(
             src_ref=nbuf.at[mine], dst_ref=nbuf.at[mine], send_sem=n_s.at[other],
-            recv_sem=n_r.at[mine], device_id=(other // parties, lax.rem(other, parties)),
+            recv_sem=n_r.at[mine], device_id=(lax.div(other, parties), lax.rem(other, parties)),
             device_id_type=MESH,
         )
 
@@ -312,7 +335,7 @@
         other = lax.rem(mine + k, total)
         return pltpu.make_async_remote_copy(
             src_ref=nbuf.at[mine], dst_ref=nbuf.at[other], send_sem=n_s.at[other],
-            recv_sem=n_r.at[other], device_id=(other // parties, lax.rem(other, parties)),
+            recv_sem=n_r.at[other], device_id=(lax.div(other, parties), lax.rem(other, parties)),
             device_id_type=MESH,
         )
 
@@ -363,7 +386,9 @@
     block = width_x * width_y
     cap = max(2 * rows // parties, 4)
     window = (2 * REACH + 1) * block
+    sources = source_cell.shape[1]
     vmem = pl.BlockSpec(memory_space=pltpu.VMEM)
+    hbm = pl.BlockSpec(memory_space=pltpu.HBM)
     dma = pltpu.SemaphoreType.DMA
     update, agreement = pl.pallas_call(
         functools.partial(kernel, parties, batches, steps, block, width_y, width_z, cap, rows),
@@ -371,9 +396,17 @@
             jax.ShapeDtypeStruct((width_x, width_y // 2, width_z), F32),
             jax.ShapeDtypeStruct((1, 128), F32),
         ),
-        in_specs=[vmem] * 7,
+        in_specs=[hbm] * 7,
         out_specs=(vmem, vmem),
         scratch_shapes=[
+            pltpu.VMEM((block, width_z), F32),
+            pltpu.VMEM((steps, 1, sources), F32),
+            pltpu.VMEM((1, sources), I32),
+            pltpu.VMEM((1, sources), I32),
+            pltpu.VMEM((steps, 1, rows), F32),
+            pltpu.VMEM((1, rows), I32),
+            pltpu.VMEM((1, rows), I32),
+            dma((7,)),
             pltpu.VMEM((8, rows), F32),
             pltpu.VMEM((parties, 8, 128), F32),
             pltpu.VMEM((parties, 8, 128), F32),
@@ -389,8 +422,8 @@
             pltpu.VMEM((2, window, width_z), BF16),
             pltpu.VMEM((2, window, width_z), BF16),
             pltpu.VMEM((steps, block, width_z), F32),
-            pltpu.VMEM((2, block, 2 * block), BF16),
-            pltpu.VMEM((2, width_z, width_z), BF16),
+            pltpu.VMEM((block, 2 * block), BF16),
+            pltpu.VMEM((width_z, width_z), BF16),
             pltpu.VMEM((2, width_x, width_y // 2, width_z), F32),
             pltpu.VMEM((width_x, width_y // 2, width_z), F32),
             pltpu.VMEM((parties * batches, 1, 128), F32),
@@ -400,14 +433,14 @@
             dma((parties * batches,)), dma((parties * batches,)),
         ],
         compiler_params=pltpu.CompilerParams(
-            collective_id=0, has_side_effects=True, vmem_limit_bytes=40 * 1024 * 1024
+            collective_id=0, has_side_effects=True, vmem_limit_bytes=64 * 1024 * 1024
         ),
     )(
         courant.reshape(block, width_z),
-        wavelet[0].T,
+        wavelet.transpose(2, 0, 1),
         source_owner,
         source_cell,
-        traces[0].T,
+        traces.transpose(2, 0, 1),
         station_owner.reshape(1, rows),
         station_cell,
     )

time: 37.9 us -> 36.7 us (0.968)
  local copies, waits for them, and re-layouts: 2.93 us -> 1.48 us
    unnamed x15 -> x3, local copies, waits for them, and re-layouts: 2.93 us -> 1.48 us
where the time goes in v2:
time: 36.7 us; the launch traced here: 36.5 us
  Pallas kernels  33.2 us (90%)
  between operations  1.81 us (5%)
  local copies, waits for them, and re-layouts  1.48 us (4%)
    pallas_call x1, Pallas kernels, body(): pl.pallas_call(functools.partial(kernel, parties, batches, steps, block,...  33.2 us
    unnamed x3, local copies, waits for them, and re-layouts  1.48 us

profile of v2, /device:TPU:0, one launch (start us, length us, event | category | flops | bytes accessed | tf_op | source)
XLA Modules:
  0.0 36.5 jit_solution(5968392405705590847)
XLA Ops:
  0.6 33.2 %shard_map.86 = (f32[8,8,256]{2,1,0:T(8,128)}, f32[1,128]{1,0:T(1,128)}) custom-call(f32[128,256]{1,0:T(8,128)} %bitcast.6, f32[7,1,64]{2,1,0:T(1,128)} %bitcast.8, s32[1,64]{1,0:T(1,128)} %s_own_in.1, s32[1,64]{1,0:T(1,128)} %s_cell_in.1, f32[7,1,256]{2,1,0:T(1,128)} %bitcast.7, s32[1,256]{1,0:T(1,128)} %bitcast.9, s32[1,256]{1,0:T(1,128)} %t_cell_in.1), custom_call_target="tpu_custom_call" | custom-call | tf_op jit(solution)/shard_map/pallas_call | solution.py:393
  33.9 0.0 copy-start
  33.9 1.5 %copy.11 = f32[8,8,256]{2,1,0:T(8,128)} copy(f32[8,8,256]{2,1,0:T(8,128)} %get-tuple-element.8) | data formatting | bytes 131072
  35.4 0.0 copy-done
Async XLA Ops:
  33.9 1.5 %copy-start = (f32[1,128]{1,0:T(1,128)S(1)}, f32[1,128]{1,0:T(1,128)}, u32[]{:S(2)}) copy-start(f32[1,128]{1,0:T(1,128)} %get-tuple-element.5) | copy-start | bytes 1540

commit v3 on v2

--- a/solution.py
+++ b/solution.py
@@ -132,18 +132,58 @@
 
     lax.fori_loop(1, parties, start_route, 0)
 
-    def cour_copy(n, hop, receiving):
-        part = block
-        lo = 0
-        if abs(hop) == REACH:
-            part = block // 2
-            lo = block // 2 if hop > 0 else 0
-        at = REACH - hop
+    side = 2 * lax.rem(me, 2) - 1
+    partner = me - side
+    half = block // 2
+    upper = half * (1 - lax.rem(me, 2))
+
+    def inside(place):
+        return (place >= 0) & (place < parties)
+
+    def block_copy(n, from_offset, to_offset, lo, count, device):
+        start_from = pl.multiple_of((REACH + from_offset) * block + lo, half)
+        start_to = pl.multiple_of((REACH + to_offset) * block + lo, half)
         return pltpu.make_async_remote_copy(
-            src_ref=cext.at[pl.ds(middle + lo, part)], dst_ref=cext.at[pl.ds(at * block + lo, part)],
-            send_sem=c_s.at[n], recv_sem=c_r.at[at],
-            device_id=(b, me - hop if receiving else me + hop), device_id_type=MESH,
-        )
+            src_ref=cext.at[pl.ds(start_from, count)], dst_ref=cext.at[pl.ds(start_to, count)],
+            send_sem=c_s.at[n], recv_sem=c_r.at[n], device_id=(b, device), device_id_type=MESH,
+        )
+
+    other_upper = half - upper
+    near = (
+        me + side, block_copy(0, 0, -side, 0, block, me + side),
+        me + side, block_copy(0, 0, side, 0, block, me + side),
+    )
+    second = (
+        me - 2 * side, block_copy(1, 0, 2 * side, 0, block, me - 2 * side),
+        me + 2 * side, block_copy(1, 0, 2 * side, 0, block, me + 2 * side),
+    )
+    third = (
+        me + 3 * side, block_copy(2, 0, -3 * side, other_upper, half, me + 3 * side),
+        me + 3 * side, block_copy(2, 0, 3 * side, upper, half, me + 3 * side),
+    )
+    twin = (
+        partner, block_copy(3, 0, side, 0, block, partner),
+        partner, block_copy(3, 0, -side, 0, block, partner),
+    )
+    onward = (
+        me + side, block_copy(4, side, 2 * side, 0, block, partner),
+        me - 2 * side, block_copy(4, 0, -2 * side, 0, block, partner),
+    )
+    onward_half = (
+        me + 2 * side, block_copy(5, 2 * side, 3 * side, upper, half, partner),
+        me - 3 * side, block_copy(5, 0, -3 * side, other_upper, half, partner),
+    )
+    all_copies = (near, second, third, twin, onward, onward_half)
+
+    def send(copy):
+        @pl.when(inside(copy[0]))
+        def _():
+            copy[1].start()
+
+    def receive(copy):
+        @pl.when(inside(copy[2]))
+        def _():
+            copy[3].wait_recv()
 
     def relay_copy(n, hop, receiving):
         at = REACH - hop
@@ -153,14 +193,9 @@
             device_id_type=MESH,
         )
 
-    def inside(place):
-        return (place >= 0) & (place < parties)
-
+    send(near)
+    send(twin)
     for n, hop in enumerate(HOPS):
-        @pl.when(inside(me + hop))
-        def _():
-            cour_copy(n, hop, False).start()
-
         at = REACH - hop
 
         @pl.when(jnp.logical_not(inside(me - hop)))
@@ -212,6 +247,11 @@
         def _():
             relay_copy(n, hop, False).start()
 
+    send(second)
+    send(third)
+    receive(near)
+    send(onward)
+
     last = steps - 1
 
     def stations(at):
@@ -227,6 +267,8 @@
             field_r[t, pl.ds(at * block, block), :] = field
 
     stations(REACH)
+    receive(second)
+    send(onward_half)
     for n, hop in enumerate(HOPS):
         @pl.when(inside(me - hop))
         def _():
@@ -235,11 +277,8 @@
         stations(REACH - hop)
 
     def wait_cour(distance):
-        for n, hop in enumerate(HOPS):
-            if abs(hop) == distance:
-                @pl.when(inside(me - hop))
-                def _():
-                    cour_copy(n, hop, True).wait_recv()
+        for copy in ((twin,), (onward,), (third, onward_half))[distance - 1]:
+            receive(copy)
 
     xy, z = taps_xy[...], taps_z[...]
 
@@ -320,6 +359,7 @@
         src_ref=gbuf.at[1 - b], dst_ref=gin, send_sem=g_s, recv_sem=g_r,
         device_id=(1 - b, me), device_id_type=MESH,
     )
+    swap.start()
     squares = jnp.sum(gradient * gradient, axis=0, keepdims=True)
     nbuf[mine] = squares[:, :128] + squares[:, 128:]
 
@@ -348,7 +388,6 @@
         return carry
 
     lax.fori_loop(1, total, start_norm, 0)
-    swap.start()
 
     def end_route(k, carry):
         route(k).wait_send()
@@ -358,8 +397,11 @@
     for n, hop in enumerate(HOPS):
         @pl.when(inside(me + hop))
         def _():
-            cour_copy(n, hop, False).wait_send()
             relay_copy(n, hop, False).wait_send()
+    for copy in all_copies:
+        @pl.when(inside(copy[0]))
+        def _():
+            copy[1].wait_send()
 
     lax.fori_loop(1, total, end_norm, 0)
     cells = float(block * width_z * parties)
@@ -428,7 +470,7 @@
             pltpu.VMEM((width_x, width_y // 2, width_z), F32),
             pltpu.VMEM((parties * batches, 1, 128), F32),
             dma((parties,)), dma((parties,)),
-            dma((6,)), dma((7,)), dma((6,)), dma((7,)),
+            dma((6,)), dma((6,)), dma((6,)), dma((7,)),
             dma, dma,
             dma((parties * batches,)), dma((parties * batches,)),
         ],

time: 36.7 us -> 34.3 us (0.935)
  Pallas kernels: 33.2 us -> 30.8 us
    pallas_call x1, Pallas kernels: 33.2 us -> 30.8 us  [body(): pl.pallas_call(functools.partial(kernel, parties, batches, steps, block,...]
where the time goes in v3:
time: 34.3 us; the launch traced here: 34.1 us
  Pallas kernels  30.8 us (90%)
  between operations  1.81 us (5%)
  local copies, waits for them, and re-layouts  1.48 us (4%)
    pallas_call x1, Pallas kernels, body(): pl.pallas_call(functools.partial(kernel, parties, batches, steps, block,...  30.8 us
    unnamed x3, local copies, waits for them, and re-layouts  1.48 us

profile of v3, /device:TPU:0, one launch (start us, length us, event | category | flops | bytes accessed | tf_op | source)
XLA Modules:
  0.0 34.1 jit_solution(4449775572264526653)
XLA Ops:
  0.6 30.8 %shard_map.86 = (f32[8,8,256]{2,1,0:T(8,128)}, f32[1,128]{1,0:T(1,128)}) custom-call(f32[128,256]{1,0:T(8,128)} %bitcast.6, f32[7,1,64]{2,1,0:T(1,128)} %bitcast.8, s32[1,64]{1,0:T(1,128)} %s_own_in.1, s32[1,64]{1,0:T(1,128)} %s_cell_in.1, f32[7,1,256]{2,1,0:T(1,128)} %bitcast.7, s32[1,256]{1,0:T(1,128)} %bitcast.9, s32[1,256]{1,0:T(1,128)} %t_cell_in.1), custom_call_target="tpu_custom_call" | custom-call | tf_op jit(solution)/shard_map/pallas_call | solution.py:435
  31.5 0.0 copy-start
  31.5 1.5 %copy.11 = f32[8,8,256]{2,1,0:T(8,128)} copy(f32[8,8,256]{2,1,0:T(8,128)} %get-tuple-element.8) | data formatting | bytes 131072
  33.0 0.0 copy-done
Async XLA Ops:
  31.5 1.5 %copy-start = (f32[1,128]{1,0:T(1,128)S(1)}, f32[1,128]{1,0:T(1,128)}, u32[]{:S(2)}) copy-start(f32[1,128]{1,0:T(1,128)} %get-tuple-element.5) | copy-start | bytes 1540

commit v4 on v3

--- a/solution.py
+++ b/solution.py
@@ -408,11 +408,11 @@
     mean_first = jnp.sum(jnp.sum(nbuf[0:parties], axis=0), axis=1, keepdims=True) / cells
     mean_second = jnp.sum(jnp.sum(nbuf[parties:total], axis=0), axis=1, keepdims=True) / cells
     scale = 1.0 / jnp.sqrt((mean_first + mean_second) / 2.0 + epsilon)
-    agr[...] = jnp.broadcast_to(
-        (mean_first + epsilon) / (mean_first + mean_second + 2.0 * epsilon), agr.shape
-    )
+    share = (mean_first + epsilon) / (mean_first + mean_second + 2.0 * epsilon)
+    agr[0:1, :] = jnp.broadcast_to(share, (1, 128))
+    agr[1:2, :] = jnp.broadcast_to(scale, (1, 128))
     swap.wait()
-    upd[...] = (gbuf[b] + gin[...]) * scale.reshape(1, 1, 1)
+    upd[...] = gbuf[b] + gin[...]
 
     def end_norm_sent(k, carry):
         norm_out(k).wait_send()
@@ -436,7 +436,7 @@
         functools.partial(kernel, parties, batches, steps, block, width_y, width_z, cap, rows),
         out_shape=(
             jax.ShapeDtypeStruct((width_x, width_y // 2, width_z), F32),
-            jax.ShapeDtypeStruct((1, 128), F32),
+            jax.ShapeDtypeStruct((2, 128), F32),
         ),
         in_specs=[hbm] * 7,
         out_specs=(vmem, vmem),
@@ -486,7 +486,7 @@
         station_owner.reshape(1, rows),
         station_cell,
     )
-    return update, agreement[0, :1]
+    return update * agreement[1, 0], agreement[0, :1]
 
 
 def solution(mesh):

time: 34.3 us -> 35.1 us (1.023)
  other arithmetic: 0 us -> 2.16 us
  between operations: 1.81 us -> 0.65 us
    mul x0 -> x1, other arithmetic: none -> 2.16 us  [body(): return (update * agreement[1, 0], agreement[0, :1])]
    unnamed x3 -> x2, local copies, waits for them, and re-layouts: 1.48 us -> 0.67 us
    slice x0 -> x1, local copies, waits for them, and re-layouts: none -> 0.6 us  [body(): return (update * agreement[1, 0], agreement[0, :1])]
where the time goes in v4:
time: 35.1 us; the launch traced here: 34.9 us
  Pallas kernels  30.8 us (88%)
  other arithmetic  2.16 us (6%)
  local copies, waits for them, and re-layouts  1.27 us (4%)
  between operations  0.65 us (2%)
    pallas_call x1, Pallas kernels, body(): pl.pallas_call(functools.partial(kernel, parties, batches, steps, block,...  30.8 us
    mul x1, other arithmetic, body(): return (update * agreement[1, 0], agreement[0, :1])  2.16 us

profile of v4, /device:TPU:0, one launch (start us, length us, event | category | flops | bytes accessed | tf_op | source)
XLA Modules:
  0.0 34.9 jit_solution(7635027393563688094)
XLA Ops:
  0.6 30.8 %shard_map.86 = (f32[8,8,256]{2,1,0:T(8,128)}, f32[2,128]{1,0:T(2,128)}) custom-call(f32[128,256]{1,0:T(8,128)} %bitcast.6, f32[7,1,64]{2,1,0:T(1,128)} %bitcast.8, s32[1,64]{1,0:T(1,128)} %s_own_in.1, s32[1,64]{1,0:T(1,128)} %s_cell_in.1, f32[7,1,256]{2,1,0:T(1,128)} %bitcast.7, s32[1,256]{1,0:T(1,128)} %bitcast.9, s32[1,256]{1,0:T(1,128)} %t_cell_in.1), custom_call_target="tpu_custom_call" | custom-call | tf_op jit(solution)/shard_map/pallas_call | solution.py:435
  31.5 0.0 copy-start
  31.5 0.7 %copy-done = f32[2,128]{1,0:T(2,128)S(1)} copy-done((f32[2,128]{1,0:T(2,128)S(1)}, f32[2,128]{1,0:T(2,128)}, u32[]{:S(2)}) %copy-start) | copy-done | bytes 1048
  32.2 0.6 %fusion = (f32[1,1]{1,0:T(1,128)}, f32[1,1]{1,0:T(1,128)}) fusion(f32[2,128]{1,0:T(2,128)S(1)} %copy-done), kind=kLoop, calls=%fused_computation.1 | loop fusion | bytes 16 | tf_op jit(solution)/shard_map/slice | solution.py:489
  32.8 2.2 %broadcast_multiply_fusion = f32[8,8,256]{2,1,0:T(8,128)} fusion(f32[8,8,256]{2,1,0:T(8,128)} %get-tuple-element.4, f32[]{:T(128)} %bitcast.4), kind=kLoop, calls=%fused_computation | loop fusion | flops 16384 | bytes 131076 | tf_op jit(solution)/shard_map/mul | solution.py:489
Async XLA Ops:
  31.5 0.7 %copy-start = (f32[2,128]{1,0:T(2,128)S(1)}, f32[2,128]{1,0:T(2,128)}, u32[]{:S(2)}) copy-start(f32[2,128]{1,0:T(2,128)} %get-tuple-element.5) | copy-start | bytes 3076
